TPU v7x, 32 devices: a whole 2x2x4 slice. The times are simulated.
32 devices in a mesh: seq: 8 (over y, x, core), head: 4 (over z).
Axes of the slice: x: 2, y: 2, z: 4, core: 2. Of those that a mesh axis runs over, the one named last changes fastest.
Arguments:
- tokens: bfloat16 [32768, 768], P(('seq', 'head')), may hold values from -6 to 6
- lengths: int32 [8, 32], P('seq'), may hold values from 1 to 512, 4096 in all within a row
- cotangent: bfloat16 [32768, 768], P(('seq', 'head')), may hold values from -12 to 12
- w_query: bfloat16 [768, 768], replicated, may hold values from -0.21875 to 0.21875
- w_key: bfloat16 [768, 768], replicated, may hold values from -0.21875 to 0.21875
- w_value: bfloat16 [768, 768], replicated, may hold values from -0.21875 to 0.21875
- w_output: bfloat16 [768, 768], replicated, may hold values from -1.25 to 1.25
- vera_down: bfloat16 [768, 1024], replicated, may hold values from -0.21875 to 0.21875
- vera_up: bfloat16 [1024, 768], replicated, may hold values from -0.1875 to 0.1875
- query_scale: float32 [1024], replicated, may hold values from 0.5 to 1.5
- query_bias: float32 [768], replicated, may hold values from -4 to 4
- value_scale: float32 [1024], replicated, may hold values from 0.5 to 1.5
- value_bias: float32 [768], replicated, may hold values from -4 to 4
- hidden_in: bfloat16 [768, 3072], P(None, ('seq', 'head')), may hold values from -0.21875 to 0.21875
- hidden_out: bfloat16 [768, 3072], P(None, ('seq', 'head')), may hold values from -0.109375 to 0.109375
Outputs:
- layer_output: bfloat16 [32768, 768], P(('seq', 'head'))
- token_grad: bfloat16 [32768, 768], P(('seq', 'head'))
- query_scale_grad: float32 [1024], replicated
- query_bias_grad: float32 [768], replicated
- value_scale_grad: float32 [1024], replicated
- value_bias_grad: float32 [768], replicated
Inputs may be any that keep to these rules, and one draw needn't show every extreme that they name: `lengths`: each row sums to 4096, and its longest sequence has exactly 512 tokens.
All inputs are finite; a program needn't handle non-finite values.
Results may differ from a plain program's by a relative error of at most 0.015.
Values may be sent and summed in bfloat16 or wider, within the bound.
A program may use at most 192 MiB of HBM per device.

v0:
```python
import functools
import math

import jax
import jax.numpy as jnp
from jax import lax
from jax.experimental import pallas as pl
from jax.experimental.pallas import tpu as pltpu
from jax.sharding import PartitionSpec as P

HEAD_DIM = 64
SEQ_MOST = 512
EPSILON = 1e-05
HIDDEN = -(2.0**100)
LN2 = math.log(2.0)
QUERY_FOLD = HEAD_DIM ** (-0.5) / LN2
TILE_Q = 256
TILE_K = 256
LANES = 128
PACK = 512
NN = (((1,), (0,)), ((), ()))
NT = (((1,), (1,)), ((), ()))
TN = (((0,), (0,)), ((), ()))
F32 = jnp.float32
BF16 = jnp.bfloat16
VMEM = pl.BlockSpec(memory_space=pltpu.VMEM)
SMEM = pl.BlockSpec(memory_space=pltpu.SMEM)
MESH = pl.DeviceIdType.MESH
ANY = pl.BlockSpec(memory_space=pl.ANY)
PARAMS = pltpu.CompilerParams(vmem_limit_bytes=58 << 20)


def dot(left, right, form):
    return lax.dot_general(left, right, form, preferred_element_type=F32)


def sds(shape, dtype):
    return jax.ShapeDtypeStruct(shape, dtype)


def span(index, size):
    if isinstance(index, int):
        return pl.ds(index * size, size)
    return pl.ds(pl.multiple_of(index * size, size), size)


def bounds(len_ref, first, count):
    row = first + lax.broadcasted_iota(jnp.int32, (1, count), 1)
    low = jnp.zeros((1, count), jnp.int32)
    high = jnp.full((1, count), 1 << 30, jnp.int32)
    end = 0
    for i in range(len_ref.shape[1]):
        end = end + len_ref[0, i]
        low = jnp.where(row >= end, end, low)
        high = jnp.where(row < end, jnp.minimum(high, end), high)
    return low, high


def fill_masks(len_ref, shift, query_mask, key_mask):
    for ref, first, within, outside in ((query_mask, shift + SEQ_MOST, HIDDEN, 0.0), (key_mask, shift, 0.0, 1.0)):
        row = first + lax.broadcasted_iota(jnp.int32, (1, ref.shape[1]), 1)
        end, pieces = 0, []
        for i in range(ref.shape[0]):
            start, end = end, end + len_ref[0, i]
            pieces.append(jnp.where((row >= start) & (row < end), within, outside))
        ref[...] = jnp.concatenate(pieces, axis=0).astype(BF16)


def reach(len_ref, first, count):
    last = first + count - 1
    end, least, most = 0, 0, 1 << 30
    for i in range(len_ref.shape[1]):
        end = end + len_ref[0, i]
        least = jnp.where(first >= end, end, least)
        most = jnp.where(last < end, jnp.minimum(most, end), most)
    return least, most


def key_range(least, most, shift):
    start = (least - shift) // LANES
    return start, (most - shift - start * LANES + LANES - 1) // LANES


def other(index, bit):
    return index + bit - 2 * bit * ((index // bit) % 2)


def remote(src, dst, send, recv, seq, head):
    return pltpu.make_async_remote_copy(
        src_ref=src, dst_ref=dst, send_sem=send, recv_sem=recv, device_id=(seq, head), device_id_type=MESH
    )


class Gather:
    def __init__(self, own, full, sems, seq, head, n_head):
        self.own, self.full, self.sems = own, full, sems
        self.seq, self.head, self.n = seq, head, n_head
        self.shard = own.shape[1]
        self.near_x, self.near_y = other(seq, 2), other(seq, 4)
        self.groups = (seq, self.near_x, self.near_y, other(self.near_x, 4))

    def origin(self, way):
        return self.head - way if way < 4 else self.head + way - 3

    def there(self, way):
        return self.head >= way if way < 4 else self.head + way - 3 < self.n

    def rows(self, seq, origin):
        return self.full.at[:, span(seq * self.n + origin, self.shard), :]

    def source(self, way):
        return self.own if way == 0 else self.rows(self.seq, self.origin(way))

    def pair(self, kind, way):
        return self.sems.at[2 * (7 * kind + way)], self.sems.at[2 * (7 * kind + way) + 1]

    def local(self):
        return pltpu.make_async_copy(self.own, self.rows(self.seq, self.head), self.sems.at[0])

    def up(self, far):
        dst = self.rows(self.seq, self.head - far)
        return remote(self.source(far), dst, self.pair(8, far)[0], self.pair(0, far + 1)[1], self.seq, self.head + 1)

    def down(self, far):
        way = far + 3 if far else 0
        dst = self.rows(self.seq, self.head + far)
        return remote(self.source(way), dst, self.pair(8, far)[1], self.pair(0, far + 4)[1], self.seq, self.head - 1)

    def came_z(self, way):
        dst = self.rows(self.seq, self.origin(way))
        return remote(dst, dst, *self.pair(0, way), self.seq, self.head)

    def over_x(self, way):
        dst = self.rows(self.seq, self.origin(way))
        return remote(self.source(way), dst, *self.pair(1, way), self.near_x, self.head)

    def over_y(self, way):
        dst = self.rows(self.seq, self.origin(way))
        return remote(self.source(way), dst, *self.pair(2, way), self.near_y, self.head)

    def onward(self, way, half):
        src, to = ((self.near_x, self.near_y), (self.near_y, self.near_x))[half]
        part = self.rows(src, self.origin(way)).at[half]
        return remote(part, part, *self.pair(3 + half, way), to, self.head)

    def across(self, group, way):
        dst = self.rows(self.groups[group], self.origin(way))
        src = self.own if group == 0 and way == 0 else dst
        sems = self.sems.at[126 + 2 * (7 * group + way)], self.sems.at[127 + 2 * (7 * group + way)]
        return remote(src, dst, *sems, other(self.seq, 1), self.head)

    def slots(self, index):
        z = self.head
        return (
            ((0, None),),
            ((1, z > 0), (4, z == 0)),
            ((4, (z == 1) | (z == 2)), (5, z == 0), (2, z == 3)),
            ((6, z == 0), (5, z == 1), (2, z == 2), (3, z == 3)),
        )[index]

    def each(self, index, action):
        for way, chosen in self.slots(index):
            if chosen is None:
                action(way)
            else:
                pl.when(chosen)(functools.partial(action, way))

    def begin(self):
        pl.when(self.head < self.n - 1)(lambda: self.up(0).start())
        pl.when(self.head > 0)(lambda: self.down(0).start())
        self.local().start()
        self.spread(0)

    def take_z(self, far):
        def below():
            self.came_z(far).wait_recv()
            if far < self.n - 1:
                pl.when(self.head < self.n - 1)(lambda: self.up(far).start())

        def above():
            self.came_z(far + 3).wait_recv()
            if far < self.n - 1:
                pl.when(self.head > 0)(lambda: self.down(far).start())

        pl.when(self.there(far))(below)
        pl.when(self.there(far + 3))(above)

    def spread(self, index):
        def action(way):
            self.over_x(way).start()
            self.over_y(way).start()
            self.across(0, way).start()

        self.each(index, action)

    def take_xy(self, index):
        def action(way):
            self.over_x(way).wait_recv()
            self.onward(way, 0).start()
            self.over_y(way).wait_recv()
            self.onward(way, 1).start()
            self.across(1, way).start()
            self.across(2, way).start()

        self.each(index, action)

    def take_far(self, index):
        def action(way):
            self.onward(way, 0).wait_recv()
            self.onward(way, 1).wait_recv()
            self.across(3, way).start()

        self.each(index, action)

    def end(self):
        self.local().wait()
        for far in range(3):
            pl.when((self.head < self.n - 1) & (self.head >= far))(lambda: self.up(far).wait_send())
            pl.when((self.head > 0) & (self.head + far < self.n))(lambda: self.down(far).wait_send())
        for way in range(7):

            def action():
                self.over_x(way).wait_send()
                self.over_y(way).wait_send()
                self.onward(way, 0).wait_send()
                self.onward(way, 1).wait_send()
                for group in range(4):
                    copy = self.across(group, way)
                    copy.wait_send()
                    copy.wait_recv()

            if way == 0:
                action()
            else:
                pl.when(self.there(way))(action)


def front_kernel(n_head, n_seq, gather, *refs):
    big, refs = refs[:6], refs[6:]
    len_ref, vectors, refs = refs[0], refs[1:5], refs[5:]
    if gather:
        (hi_ref, ho_ref), refs = refs[:2], refs[2:]
    (ct_ref, ls_ref), refs = refs[:2], refs[2:]
    stored, refs = refs[:8], refs[8:]
    if gather:
        full_ref, refs = refs[0], refs[1:]
    held, refs = refs[:6], refs[6:]
    kept, refs = refs[:8], refs[8:]
    (
        xl_ref, xr_ref, acc_ref, high_ref, total_ref, query_mask, key_mask,
        load_sem, store_sem, halo_sem,
    ), refs = refs[:10], refs[10:]
    x_hbm = big[0]
    loads = [pltpu.make_async_copy(src, dst, load_sem.at[n]) for n, (src, dst) in enumerate(zip(big, held))]
    stores = [pltpu.make_async_copy(src, dst, store_sem.at[n]) for n, (src, dst) in enumerate(zip(kept, stored))]
    for n in (1, 2, 3, 4, 0, 5):
        loads[n].start()
    x_ref, down_ref, up_ref, wq_ref, wv_ref, wk_ref = held
    qt_ref, ke_ref, ve_ref, xt_ref, lt_ref, rt_ref, wqe_ref, wve_ref = kept
    rows, width = x_ref.shape
    heads = width // HEAD_DIM
    seq, head_at = lax.axis_index("seq"), lax.axis_index("head")
    shift = head_at * rows - SEQ_MOST
    first_z, last_z = head_at == 0, head_at == n_head - 1

    barrier = pltpu.get_barrier_semaphore()
    partners = [(seq, (head_at + k) % n_head) for k in range(1, n_head)]
    if gather:
        partners += [(other(seq, bit), head_at) for bit in (1, 2, 4)]
        own_ref, gather_sem = refs
        own_ref[0] = hi_ref[...]
        own_ref[1] = ho_ref[...]
    for partner in partners:
        pl.semaphore_signal(barrier, inc=1, device_id=partner, device_id_type=MESH)
    pl.semaphore_wait(barrier, len(partners))

    half = SEQ_MOST // 2

    def to_right(far):
        at = 0 if far else half
        sems = halo_sem.at[4 * far], halo_sem.at[4 * far + 1]
        src = x_hbm.at[pl.ds(rows - SEQ_MOST + at, half)]
        return remote(src, xl_ref.at[pl.ds(at, half)], *sems, seq, (head_at + 1) % n_head)

    def to_left(far):
        at = half if far else 0
        sems = halo_sem.at[4 * far + 2], halo_sem.at[4 * far + 3]
        src = x_hbm.at[pl.ds(at, half)]
        return remote(src, xr_ref.at[pl.ds(at, half)], *sems, seq, (head_at + n_head - 1) % n_head)

    def send_halo(far):
        pl.when(head_at < n_head - 1)(lambda: to_right(far).start())
        pl.when(head_at > 0)(lambda: to_left(far).start())

    if gather:
        g = Gather(own_ref, full_ref, gather_sem, seq, head_at, n_head)
        g.begin()
    else:
        send_halo(0)
        send_halo(1)
    query_scale, query_bias, value_scale, value_bias = [ref[...].reshape(1, -1) for ref in vectors]
    for n in (1, 2, 3, 4):
        loads[n].wait()

    def fold(index, carry):
        part = span(index, 256)
        down = down_ref[part, :].astype(F32)
        side_q = dot((down * query_scale).astype(BF16), up_ref[...], NN) * query_bias
        wqe_ref[part, :] = ((wq_ref[part, :].astype(F32) + side_q) * QUERY_FOLD).astype(BF16)
        side_v = dot((down * value_scale).astype(BF16), up_ref[...], NN) * value_bias
        wve_ref[part, :] = (wv_ref[part, :].astype(F32) + side_v).astype(BF16)
        return carry

    lax.fori_loop(0, width // 256, fold, 0)
    stores[6].start()
    stores[7].start()
    loads[0].wait()

    def flip(index, carry):
        part = span(index, 256)
        xt_ref[:, part] = x_ref[part, :].T
        return carry

    lax.fori_loop(0, rows // 256, flip, 0)
    stores[3].start()
    own = slice(SEQ_MOST, SEQ_MOST + rows)

    def apply(weight_ref, out_ref, at):
        def piece(index, carry):
            part = span(index, 256)
            out_ref[part, at] = dot(weight_ref[:, part], xt_ref[...], TN).astype(BF16)
            return carry

        lax.fori_loop(0, width // 256, piece, 0)

    apply(wqe_ref, qt_ref, slice(0, rows))
    if gather:
        g.take_z(1)
        g.spread(1)
    loads[5].wait()
    stores[0].start()
    apply(wk_ref, ke_ref, own)
    apply(wve_ref, ve_ref, own)

    fill_masks(len_ref, shift, query_mask, key_mask)
    acc_ref[...] = jnp.zeros_like(acc_ref)
    high_ref[...] = jnp.full_like(high_ref, HIDDEN)
    total_ref[...] = jnp.zeros_like(total_ref)

    def block(tile, key_tile):
        q_part, k_part = span(tile, TILE_Q), span(key_tile, TILE_K)
        q_mask, k_mask = query_mask[:, q_part], key_mask[:, k_part]
        parts = [span(head, HEAD_DIM) for head in range(heads)]
        before = [high_ref[head, :, q_part] for head in range(heads)]
        totals = [total_ref[head, :, q_part] for head in range(heads)]
        sums = [acc_ref[part, q_part] for part in parts]
        scores = [
            dot(
                jnp.concatenate([ke_ref[part, k_part], k_mask]),
                jnp.concatenate([qt_ref[part, q_part], q_mask]),
                TN,
            )
            for part in parts
        ]
        best = [jnp.maximum(b, jnp.max(v, axis=0, keepdims=True)) for b, v in zip(before, scores)]
        probs = [jnp.exp2(v - b) for v, b in zip(scores, best)]
        fade = [jnp.exp2(a - b) for a, b in zip(before, best)]
        totals = [t * f + jnp.sum(p, axis=0, keepdims=True) for t, f, p in zip(totals, fade, probs)]
        sums = [
            a * f + dot(ve_ref[part, k_part], p.astype(BF16), NN)
            for a, f, p, part in zip(sums, fade, probs, parts)
        ]
        for head, part, b, t, a in zip(range(heads), parts, best, totals, sums):
            high_ref[head, :, q_part] = b
            total_ref[head, :, q_part] = t
            acc_ref[part, q_part] = a

    steps = {}
    if gather:
        steps = {
            0: lambda: (g.take_xy(0),),
            2: lambda: (g.take_z(2), g.spread(2),),
            3: lambda: (send_halo(0),),
            4: lambda: (g.take_xy(1),),
            7: lambda: (g.take_z(3), g.spread(3), g.take_far(0),),
            8: lambda: (send_halo(1),),
            10: lambda: (g.take_xy(2),),
            12: lambda: (g.take_far(1),),
            15: lambda: (g.take_xy(3),),
            16: lambda: (g.take_far(2),),
            19: lambda: (g.take_far(3),),
        }

    def blocks(first, last, place):
        def one(index, carry):
            for at in steps:
                if first <= at < last:

                    @pl.when(index == at)
                    def _():
                        steps[at]()

            block(*place(index))
            return carry

        lax.fori_loop(first, last, one, 0)

    def own_place(index):
        tile = (index + 1) // 4
        return tile, (index + 1) % 4 + 1 + (tile + 1) // 2

    blocks(0, 14, own_place)

    def take_halo(far):
        for absent, copy, side_ref, flat_ref, base, at in (
            (first_z, to_right(far), xl_ref, lt_ref, 0, 0 if far else half),
            (last_z, to_left(far), xr_ref, rt_ref, SEQ_MOST + rows, half if far else 0),
        ):
            piece, place = slice(at, at + half), slice(base + at, base + at + half)

            @pl.when(absent)
            def _():
                side_ref[piece, :] = jnp.zeros((half, width), BF16)

            pl.when(jnp.logical_not(absent))(copy.wait_recv)
            flat_ref[:, piece] = side_ref[piece, :].T

            def edge(index, carry):
                part = span(index, 256)
                ke_ref[part, place] = dot(wk_ref[:, part], flat_ref[:, piece], TN).astype(BF16)
                ve_ref[part, place] = dot(wve_ref[:, part], flat_ref[:, piece], TN).astype(BF16)
                return carry

            lax.fori_loop(0, width // 256, edge, 0)

    take_halo(0)
    blocks(14, 18, lambda index: (index - 14, 1 + 5 * ((index - 14) // 2)))
    take_halo(1)
    for n in (1, 2, 4, 5):
        stores[n].start()
    blocks(18, 20, lambda index: (3 * (index - 18), 7 * (index - 18)))

    for head in range(heads):
        part = pl.ds(head * HEAD_DIM, HEAD_DIM)
        total = total_ref[head]
        ct_ref[part, :] = (acc_ref[part, :] / total).astype(BF16)
        ls_ref[head] = high_ref[head] + jnp.log2(total)

    for far in range(2):
        pl.when(head_at < n_head - 1)(to_right(far).wait_send)
        pl.when(head_at > 0)(to_left(far).wait_send)
    for store in stores:
        store.wait()
    if gather:
        g.end()


def attend_back_kernel(
    len_ref, qt_hbm, ke_hbm, ve_hbm, ls_ref, gt_hbm, dl_ref,
    dq_hbm, dk_hbm, dv_hbm,
    qt_ref, ke_ref, ve_ref, gt_ref, dq_ref, dk_ref, dv_ref,
    dq_acc, dk_acc, dv_acc, bias_ref, load_sem, store_sem,
):
    width, rows = qt_ref.shape
    extent = ke_ref.shape[1]
    heads = width // HEAD_DIM
    shift = lax.axis_index("head") * rows - SEQ_MOST
    loads = [
        pltpu.make_async_copy(src, dst, load_sem.at[n])
        for n, (src, dst) in enumerate(((ke_hbm, ke_ref), (qt_hbm, qt_ref), (ve_hbm, ve_ref), (gt_hbm, gt_ref)))
    ]
    for load in loads:
        load.start()

    def store(kind, tile):
        src, dst = ((dq_ref, dq_hbm), (dk_ref, dk_hbm), (dv_ref, dv_hbm))[kind]
        part = span(tile, TILE_Q)
        return pltpu.make_async_copy(src.at[:, part], dst.at[:, part], store_sem.at[kind, tile])

    def settle(tile, carry):
        part = span(tile, TILE_Q)
        dk_ref[:, part] = (dk_acc[:, part] * LN2).astype(BF16)
        dv_ref[:, part] = dv_acc[:, part].astype(BF16)
        store(1, tile).start()
        store(2, tile).start()
        return carry

    dk_acc[...] = jnp.zeros_like(dk_acc)
    dv_acc[...] = jnp.zeros_like(dv_acc)
    for load in loads:
        load.wait()

    def query_tile(tile, carry):
        first = shift + SEQ_MOST + tile * TILE_Q
        low, high = bounds(len_ref, first, TILE_Q)
        least, most = reach(len_ref, first, TILE_Q)
        start, count = key_range(least, most, shift)
        q_part = span(tile, TILE_Q)
        dq_acc[...] = jnp.zeros_like(dq_acc)

        def keys(column, size):
            base = pl.multiple_of(column * LANES, LANES)
            k_part = pl.ds(base, size)
            key = shift + base + lax.broadcasted_iota(jnp.int32, (size, TILE_Q), 0)
            bias_ref[:size, :] = jnp.where((key >= low) & (key < high), 0.0, HIDDEN)

            def group(index):
                heads_of = [index * 6 + sub for sub in range(6)]
                parts = [span(head, HEAD_DIM) for head in heads_of]
                bias = bias_ref[:size, :]
                scores = [dot(ke_ref[part, k_part], qt_ref[part, q_part], TN) + bias for part in parts]
                grad_probs = [dot(ve_ref[part, k_part], gt_ref[part, q_part], TN) for part in parts]
                probs = [jnp.exp2(v - ls_ref[head, :, q_part]) for head, v in zip(heads_of, scores)]
                slopes = [
                    (p * (g - dl_ref[head, :, q_part])).astype(BF16)
                    for head, p, g in zip(heads_of, probs, grad_probs)
                ]
                for part, p, d in zip(parts, probs, slopes):
                    dv_acc[part, k_part] += dot(gt_ref[part, q_part], p.astype(BF16), NT)
                    dk_acc[part, k_part] += dot(qt_ref[part, q_part], d, NT)
                    dq_acc[part, :] += dot(ke_ref[part, k_part], d, NN)

            if size == TILE_K:
                for index in range(heads // 6):
                    group(index)
            else:
                lax.fori_loop(0, heads // 6, lambda index, carry: group(index), None)

        def key_tile(step, inner):
            keys(start + step * (TILE_K // LANES), TILE_K)
            return inner

        lax.fori_loop(0, count // (TILE_K // LANES), key_tile, 0)
        pl.when(count % (TILE_K // LANES) == 1)(lambda: keys(start + count - 1, LANES))
        dq_ref[:, q_part] = (dq_acc[...] * LN2).astype(BF16)
        store(0, tile).start()
        settle(tile, 0)
        return carry

    def drain(tile, carry):
        store(1, tile).wait()
        store(2, tile).wait()
        return carry

    lax.fori_loop(0, rows // TILE_Q, query_tile, 0)
    lax.fori_loop(rows // TILE_Q, extent // TILE_Q, settle, 0)
    for tile in range(rows // TILE_Q):
        store(0, tile).wait()
    lax.fori_loop(0, extent // TILE_Q, drain, 0)


def norm(values):
    center = values - jnp.mean(values, axis=0, keepdims=True)
    inverse = lax.rsqrt(jnp.mean(center * center, axis=0, keepdims=True) + EPSILON)
    return center * inverse, inverse


def norm_back(gradient, normed, inverse):
    centered = gradient - jnp.mean(gradient, axis=0, keepdims=True)
    return inverse * (centered - normed * jnp.mean(gradient * normed, axis=0, keepdims=True))


def gelu_parts(x):
    bell = jnp.exp2((-0.5 / LN2) * (x * x))
    t = 1.0 / (1.0 + (0.3275911 * math.sqrt(0.5)) * jnp.abs(x))
    poly = t * (0.127414796 + t * (-0.142248368 + t * (0.710706870 + t * (-0.726576013 + t * 0.530702714))))
    tail = poly * bell
    normal = jnp.where(x >= 0, 1.0 - tail, tail)
    return x * normal, normal + x * (bell * (1.0 / math.sqrt(2.0 * math.pi)))


def feed_kernel(
    xt_ref, ct_ref, cot_ref, wo_ref, w_ref,
    out_ref, gf_ref, gc_ref, dl_ref,
    normed_ref, low_ref, slope_ref, sum_ref, act_ref, pre_ref,
):
    width = xt_ref.shape[0]
    hidden = w_ref.shape[1]
    step = act_ref.shape[1]
    heads = width // HEAD_DIM
    pieces = [pl.ds(at, step) for at in range(0, hidden, step)]

    def sweep(first, second, change):
        count = len(pieces)
        pre_ref[0] = dot(w_ref[first, pieces[0], :], low_ref[...], NN)
        for at in range(count):
            if at + 1 < count:
                pre_ref[(at + 1) % 2] = dot(w_ref[first, pieces[at + 1], :], low_ref[...], NN)
            act_ref[at % 2] = change(pieces[at], pre_ref[at % 2]).astype(BF16)
            if at > 0:
                sum_ref[...] += dot(w_ref[second, pieces[at - 1], :], act_ref[(at - 1) % 2], TN)
        sum_ref[...] += dot(w_ref[second, pieces[-1], :], act_ref[(count - 1) % 2], TN)

    def forward(piece, pre):
        act, slope = gelu_parts(pre)
        slope_ref[piece, :] = slope
        return act

    attended = dot(wo_ref[...], ct_ref[...], TN)
    normed, inverse_first = norm(xt_ref[...].astype(F32) + attended)
    normed_ref[...] = normed
    low_ref[...] = normed.astype(BF16)
    sum_ref[...] = normed
    sweep(0, 1, forward)
    layer_out, inverse_second = norm(sum_ref[...])
    out_ref[...] = layer_out.T.astype(BF16)
    grad = norm_back(cot_ref[...].astype(F32).T, layer_out, inverse_second)
    sum_ref[...] = grad
    low_ref[...] = grad.astype(BF16)
    sweep(1, 0, lambda piece, upstream: slope_ref[piece, :] * upstream)
    grad_first = norm_back(sum_ref[...], normed_ref[...], inverse_first)
    gf_ref[...] = grad_first
    grad_context = dot(wo_ref[...], grad_first.astype(BF16), NN).astype(BF16)
    gc_ref[...] = grad_context
    product = grad_context.astype(F32) * ct_ref[...].astype(F32)
    for head in range(heads):
        dl_ref[head] = jnp.sum(
            product[head * HEAD_DIM : (head + 1) * HEAD_DIM], axis=0, keepdims=True
        )


def pack(rows):
    places, at = [], 0
    for size in rows:
        places.append([(at + n, n * PACK, min(PACK, size - n * PACK)) for n in range(-(-size // PACK))])
        at += len(places[-1])
    return places, at


def tail_kernel(n_head, n_seq, *refs):
    big, refs = refs[:12], refs[12:]
    vectors, refs = refs[:4], refs[4:]
    query_scale, query_bias, value_scale, value_bias = [ref[...].reshape(1, -1) for ref in vectors]
    (own_hbm, from_left, from_right, sum_ref), refs = refs[:4], refs[4:]
    held, refs = refs[:12], refs[12:]
    (
        load_sem, own_ref, mix_ref, send_left, send_right, halo_sem, z_slots, s_slots, z_sem, s_sem,
    ) = refs
    dk_ref, dv_ref, wk_ref, wve_ref, xt_ref, dq_ref, lt_ref, rt_ref, down_ref, up_ref, wqe_ref, gf_ref = held
    width, rows = dq_ref.shape
    rank = up_ref.shape[0]
    own = slice(SEQ_MOST, SEQ_MOST + rows)
    sides = (slice(0, SEQ_MOST), slice(SEQ_MOST + rows, 2 * SEQ_MOST + rows))
    pieces = [(wk_ref, big[2]), (wve_ref, big[3])]
    pieces += [(ref.at[:, side], hbm.at[:, side]) for side in sides for ref, hbm in zip(held[:2], big[:2])]
    pieces += [(dq_ref, big[5]), (xt_ref, big[4]), (down_ref, big[8]), (up_ref, big[9])]
    pieces += [(lt_ref, big[6]), (rt_ref, big[7]), (dv_ref.at[:, own], big[1].at[:, own])]
    pieces += [(dk_ref.at[:, own], big[0].at[:, own]), (wqe_ref, big[10]), (gf_ref, big[11])]
    loads = [pltpu.make_async_copy(src, dst, load_sem.at[n]) for n, (dst, src) in enumerate(pieces)]
    for load in loads[:6]:
        load.start()
    seq, head_at = lax.axis_index("seq"), lax.axis_index("head")

    barrier = pltpu.get_barrier_semaphore()
    partners = [(seq, (head_at + k) % n_head) for k in range(1, n_head)]
    partners += [((seq + k) % n_seq, head_at) for k in range(1, n_seq)]
    for partner in partners:
        pl.semaphore_signal(barrier, inc=1, device_id=partner, device_id_type=MESH)
    pl.semaphore_wait(barrier, len(partners))
    first_z, last_z = head_at == 0, head_at == n_head - 1

    def to_left(piece):
        part = span(piece, 256)
        sems = halo_sem.at[2 * piece], halo_sem.at[2 * piece + 1]
        return remote(
            send_left.at[:, part], from_right.at[:, part], *sems, seq, (head_at + n_head - 1) % n_head
        )

    def to_right(piece):
        part = span(piece, 256)
        piece += width // 256
        sems = halo_sem.at[2 * piece], halo_sem.at[2 * piece + 1]
        return remote(send_right.at[:, part], from_left.at[:, part], *sems, seq, (head_at + 1) % n_head)

    for load in loads[:6]:
        load.wait()
    for load in loads[6:]:
        load.start()
    for piece in range(width // 256):
        part = span(piece, 256)
        for side_ref, side, absent, copy in (
            (send_left, sides[0], first_z, to_left(piece)),
            (send_right, sides[1], last_z, to_right(piece)),
        ):
            partial = dot(wk_ref[part, :], dk_ref[:, side], NN) + dot(wve_ref[part, :], dv_ref[:, side], NN)
            side_ref[:, part] = partial.astype(BF16).T
            pl.when(jnp.logical_not(absent))(copy.start)

    places, depth = pack((rank, width, rank, width))
    s_slots[seq] = jnp.zeros_like(s_slots[0])
    for load in loads[6:10]:
        load.wait()

    for value in (False, True):
        scale_row, bias = (value_scale, value_bias) if value else (query_scale, query_bias)
        factor = 1.0 if value else QUERY_FOLD
        scale_at, bias_at = places[2 * value], places[2 * value + 1]

        if value:
            for load in loads[10:13]:
                load.wait()

        def outer(index, carry):
            part = span(index, 256)
            if value:
                total = dot(xt_ref[part, :], dv_ref[:, own], NT)
                total += dot(lt_ref[part, :], dv_ref[:, :SEQ_MOST], NT)
                total += dot(rt_ref[part, :], dv_ref[:, SEQ_MOST + rows :], NT)
            else:
                total = dot(xt_ref[part, :], dq_ref[...], NT)
            mix_ref[part, :] = total.astype(BF16)
            return carry

        lax.fori_loop(0, width // 256, outer, 0)
        bias_sum = jnp.zeros((1, width), F32)
        for at in range(0, rank, 256):
            part = slice(at, at + 256)
            mixed = dot(down_ref[:, part], mix_ref[...], TN) * up_ref[part, :].astype(F32) * factor
            scale = jnp.broadcast_to(scale_row[:, part], (LANES, 256)).T[:, :1]
            bias_sum += jnp.sum(mixed * scale, axis=0, keepdims=True)
            weighted = mixed * bias
            folded = weighted[:, :LANES]
            for lane in range(LANES, width, LANES):
                folded = folded + weighted[:, lane : lane + LANES]
            row, column = at // PACK, at % PACK
            s_slots[seq, pl.ds(scale_at[row][0], 1), pl.ds(column, 256)] = jnp.sum(
                folded.T, axis=0, keepdims=True
            )
        for row, start, size in bias_at:
            s_slots[seq, pl.ds(row, 1), pl.ds(0, size)] = bias_sum[:, start : start + size]

    def over_z(k):
        return remote(
            z_slots.at[head_at], z_slots.at[head_at], z_sem.at[2 * k], z_sem.at[2 * k + 1],
            seq, (head_at + k) % n_head,
        )

    def over_seq(k):
        return remote(
            s_slots.at[seq], s_slots.at[seq], s_sem.at[2 * k], s_sem.at[2 * k + 1],
            (seq + k) % n_seq, head_at,
        )

    for k in range(1, n_seq):
        over_seq(k).start()
    for load in loads[13:]:
        load.wait()

    def tokens_part(index, carry):
        part = span(index, 256)
        total = (
            gf_ref[part, :]
            + dot(wqe_ref[part, :], dq_ref[...], NN)
            + dot(wk_ref[part, :], dk_ref[:, own], NN)
            + dot(wve_ref[part, :], dv_ref[:, own], NN)
        )
        own_ref[:, part] = total.astype(BF16).T
        return carry

    lax.fori_loop(0, width // 256, tokens_part, 0)
    for k in range(1, n_seq):
        over_seq(k).wait_recv()
    total = s_slots[0]
    for k in range(1, n_seq):
        total = total + s_slots[k]
    z_slots[head_at] = total
    for k in range(1, n_head):
        over_z(k).start()

    out = pltpu.make_async_copy(own_ref, own_hbm, load_sem.at[len(pieces)])
    out.start()
    for k in range(1, n_head):
        over_z(k).wait_recv()
    total = z_slots[0]
    for k in range(1, n_head):
        total = total + z_slots[k]
    sum_ref[...] = total
    for absent, back, copy in ((first_z, to_right, to_left), (last_z, to_left, to_right)):

        @pl.when(jnp.logical_not(absent))
        def _():
            for piece in range(width // 256):
                back(piece).wait_recv()
                copy(piece).wait_send()

    out.wait()
    for k in range(1, n_head):
        over_z(k).wait_send()
    for k in range(1, n_seq):
        over_seq(k).wait_send()


def finish_kernel(n_head, own_ref, left_ref, right_ref, sum_ref, out_ref, *vector_refs):
    tile, last = pl.program_id(0), pl.num_programs(0) - 1
    to_first = (tile == 0) & (lax.axis_index("head") > 0)
    to_last = (tile == last) & (lax.axis_index("head") < n_head - 1)
    total = own_ref[...].astype(F32) + jnp.where(to_first, left_ref[...].astype(F32), 0.0)
    out_ref[...] = (total + jnp.where(to_last, right_ref[...].astype(F32), 0.0)).astype(BF16)

    @pl.when(tile == 0)
    def _():
        places, _ = pack([ref.shape[0] for ref in vector_refs])
        for vector_ref, place in zip(vector_refs, places):
            for row, start, size in place:
                vector_ref[start : start + size] = sum_ref[row, :size]


def call(kernel, outs, count, scratch=(), scalars=0):
    return pl.pallas_call(
        kernel,
        out_shape=outs,
        in_specs=[SMEM] * scalars + [VMEM] * count,
        out_specs=[VMEM] * len(outs),
        scratch_shapes=list(scratch),
        compiler_params=PARAMS,
    )


def front(n_head, n_seq, lengths, tokens, w_query, w_key, w_value, vera, shards):
    rows, width = tokens.shape
    heads = width // HEAD_DIM
    extent = rows + 2 * SEQ_MOST
    tall, wide = sds((width, rows), BF16), sds((width, extent), BF16)
    square, half = sds((width, width), BF16), sds((width, SEQ_MOST), BF16)
    kept = [tall, wide, wide, tall, half, half, square, square]
    outs = [tall, sds((heads, 1, rows), F32)] + kept
    big = (tokens, vera[0], vera[1], w_query, w_value, w_key)
    scratch = [pltpu.VMEM(a.shape, a.dtype) for a in (*big, *kept)] + [
        pltpu.VMEM((SEQ_MOST, width), BF16),
        pltpu.VMEM((SEQ_MOST, width), BF16),
        pltpu.VMEM((width, rows), F32),
        pltpu.VMEM((heads, 1, rows), F32),
        pltpu.VMEM((heads, 1, rows), F32),
        pltpu.VMEM((lengths.shape[1], rows), BF16),
        pltpu.VMEM((lengths.shape[1], extent), BF16),
        pltpu.SemaphoreType.DMA((len(big),)),
        pltpu.SemaphoreType.DMA((len(kept),)),
        pltpu.SemaphoreType.DMA((8,)),
    ]
    gather = len(shards) > 0
    specs = [VMEM] * 2 + [ANY] * len(kept)
    if gather:
        shard = shards[0].shape[0]
        outs.append(sds((2, n_head * n_seq * shard, width), BF16))
        specs.append(ANY)
        scratch += [pltpu.VMEM((2, shard, width), BF16), pltpu.SemaphoreType.DMA((182,))]
    return pl.pallas_call(
        functools.partial(front_kernel, n_head, n_seq, gather),
        out_shape=outs,
        in_specs=[ANY] * len(big) + [SMEM] + [VMEM] * (4 + len(shards)),
        out_specs=specs,
        scratch_shapes=scratch,
        compiler_params=pltpu.CompilerParams(
            vmem_limit_bytes=58 << 20, collective_id=0, has_side_effects=True
        ),
    )(*big, lengths, *vera[2:], *shards)


def feed(xt, ct, cotangent, w_output, weights):
    width, rows = xt.shape
    hidden = weights.shape[1]
    heads = width // HEAD_DIM
    tile, step = 512, 768
    column = pl.BlockSpec((width, tile), lambda i: (0, i))
    row = pl.BlockSpec((tile, width), lambda i: (i, 0))
    return pl.pallas_call(
        feed_kernel,
        grid=(rows // tile,),
        out_shape=[
            sds((rows, width), BF16), sds((width, rows), F32), sds((width, rows), BF16),
            sds((heads, 1, rows), F32),
        ],
        in_specs=[column, column, row, VMEM, VMEM],
        out_specs=[row, column, column, pl.BlockSpec((heads, 1, tile), lambda i: (0, 0, i))],
        scratch_shapes=[
            pltpu.VMEM((width, tile), F32),
            pltpu.VMEM((width, tile), BF16),
            pltpu.VMEM((hidden, tile), F32),
            pltpu.VMEM((width, tile), F32),
            pltpu.VMEM((2, step, tile), BF16),
            pltpu.VMEM((2, step, tile), F32),
        ],
        compiler_params=PARAMS,
    )(xt, ct, cotangent, w_output, weights)


def attend_back(lengths, qt, ke, ve, ls, gc, dl):
    width, rows = qt.shape
    extent = ke.shape[1]
    outs = [sds((width, rows), BF16), sds(ke.shape, BF16), sds(ke.shape, BF16)]
    return pl.pallas_call(
        attend_back_kernel,
        out_shape=outs,
        in_specs=[SMEM, ANY, ANY, ANY, VMEM, ANY, VMEM],
        out_specs=[ANY] * 3,
        scratch_shapes=[pltpu.VMEM(a.shape, BF16) for a in (qt, ke, ve, gc, *outs)]
        + [
            pltpu.VMEM((width, TILE_Q), F32),
            pltpu.VMEM((width, extent), F32),
            pltpu.VMEM((width, extent), F32),
            pltpu.VMEM((TILE_K, TILE_Q), F32),
            pltpu.SemaphoreType.DMA((4,)),
            pltpu.SemaphoreType.DMA((3, extent // TILE_Q)),
        ],
        compiler_params=PARAMS,
    )(lengths, qt, ke, ve, ls, gc, dl)


def tail(n_head, n_seq, big, small):
    dq, up = big[5], big[9]
    width, rows = dq.shape
    rank = up.shape[0]
    sizes = (rank, width, rank, width)
    depth = -(-pack(sizes)[1] // 8) * 8
    half = sds((SEQ_MOST, width), BF16)
    outs = [sds((rows, width), BF16), half, half, sds((depth, PACK), F32)]
    own, left, right, total = pl.pallas_call(
        functools.partial(tail_kernel, n_head, n_seq),
        out_shape=outs,
        in_specs=[ANY] * len(big) + [VMEM] * len(small),
        out_specs=[ANY] * 3 + [VMEM],
        scratch_shapes=[pltpu.VMEM(a.shape, a.dtype) for a in big]
        + [
            pltpu.SemaphoreType.DMA((17,)),
            pltpu.VMEM((rows, width), BF16),
            pltpu.VMEM((width, width), BF16),
            pltpu.VMEM(half.shape, BF16),
            pltpu.VMEM(half.shape, BF16),
            pltpu.SemaphoreType.DMA((4 * (width // 256),)),
            pltpu.VMEM((n_head, depth, PACK), F32),
            pltpu.VMEM((n_seq, depth, PACK), F32),
            pltpu.SemaphoreType.DMA((2 * n_head,)),
            pltpu.SemaphoreType.DMA((2 * n_seq,)),
        ],
        compiler_params=pltpu.CompilerParams(
            vmem_limit_bytes=58 << 20, collective_id=1, has_side_effects=True
        ),
    )(*big, *small)
    piece = pl.BlockSpec((SEQ_MOST, width), lambda i: (i, 0))
    return pl.pallas_call(
        functools.partial(finish_kernel, n_head),
        grid=(rows // SEQ_MOST,),
        out_shape=[sds((rows, width), BF16)] + [sds((size,), F32) for size in sizes],
        in_specs=[piece, VMEM, VMEM, VMEM],
        out_specs=[piece] + [VMEM] * 4,
        compiler_params=PARAMS,
    )(own, left, right, total)


def body(n_seq, n_head, *arrays):
    (
        tokens, lengths, cotangent, w_query, w_key, w_value, w_output, vera_down, vera_up,
        query_scale, query_bias, value_scale, value_bias, hidden_in, hidden_out,
    ) = arrays
    rows, width = tokens.shape
    vera = (vera_down, vera_up, query_scale, query_bias, value_scale, value_bias)
    fused = (n_seq, n_head) == (8, 4)
    shards = (hidden_in.T, hidden_out.T) if fused else ()
    ct, ls, qt, ke, ve, xt, lt, rt, wqe, wve, *full = front(
        n_head, n_seq, lengths, tokens, w_query, w_key, w_value, vera, shards
    )
    if fused:
        (weights,) = full
    else:
        weights = lax.all_gather(
            jnp.stack([hidden_in.T, hidden_out.T]), ("seq", "head"), axis=1, tiled=True
        )
    layer_out, gf, gc, dl = feed(xt, ct, cotangent, w_output, weights)
    dq, dk, dv = attend_back(lengths, qt, ke, ve, ls, gc, dl)
    token_grad, *totals = tail(
        n_head, n_seq, (dk, dv, w_key, wve, xt, dq, lt, rt, vera_down, vera_up, wqe, gf), vera[2:]
    )
    return (layer_out, token_grad, *totals)


def solution(mesh):
    return jax.shard_map(
        functools.partial(body, mesh.shape["seq"], mesh.shape["head"]),
        mesh=mesh,
        in_specs=(
            P(("seq", "head"), None),
            P("seq", None),
            P(("seq", "head"), None),
            P(), P(), P(), P(), P(), P(), P(), P(), P(), P(),
            P(None, ("seq", "head")),
            P(None, ("seq", "head")),
        ),
        out_specs=(P(("seq", "head"), None), P(("seq", "head"), None), P(), P(), P(), P()),
        check_vma=False,
    )
```

profile of v0, /device:TPU:0, one launch (start us, length us, event | category | flops | bytes accessed | tf_op | source)
XLA Modules:
  0.0 158.2 jit_solution(1681480478896227787)
XLA Ops:
  0.6 57.3 %shard_map.190 = (bf16[768,1024]{1,0:T(8,128)(2,1)}, f32[12,1,1024]{2,1,0:T(1,128)}, bf16[768,1024]{1,0:T(8,128)(2,1)}, bf16[768,2048]{1,0:T(8,128)(2,1)}, bf16[...) custom-call(bf16[1024,768]{1,0:T(8,128)(2,1)} %refs_0_.1, ...), custom_call_target="tpu_custom_call" | custom-call | tf_op jit(solution)/shard_map/pallas_call | solution.py:847
  57.9 36.7 %shard_map.191 = (bf16[1024,768]{1,0:T(8,128)(2,1)}, f32[768,1024]{1,0:T(8,128)}, bf16[768,1024]{1,0:T(8,128)(2,1)}, f32[12,1,1024]{2,1,0:T(1,128)}) custom-call(bf16[768,1024]{1,0:T(8,128)(2,1)} %get-tuple-element.33.xt_ref.refs_4_, bf16[768,1024]{1,0:T(8,128)(2,1)} %get-tuple-element.34.ct_ref, bf16[1024,768]{1,0:T(8,128)(2,1)} %cot_ref.1, ...), custom_call_target="tpu_custom_call" | custom-call | tf_op jit(solution)/shard_map/pallas_call | solution.py:866
  94.6 30.3 %shard_map.192 = (bf16[768,1024]{1,0:T(8,128)(2,1)}, bf16[768,2048]{1,0:T(8,128)(2,1)}, bf16[768,2048]{1,0:T(8,128)(2,1)}) custom-call(s32[1,32]{1,0:T(1,128)} %len_ref.1, bf16[768,1024]{1,0:T(8,128)(2,1)} %get-tuple-element.37.qt_hbm, bf16[768,2048]{1,0:T(8,128)(2,1)} %get-tuple-element.38.ke_hbm, bf16[768,2048]{1,0:T(8,128)(2,1)} %get-tuple-element.39.ve_hbm, ...), custom_call_target="tpu_custom_call" | custom-call | tf_op jit(solution)/shard_map/pallas_call | solution.py:891
  124.9 29.9 %shard_map.193 = (bf16[1024,768]{1,0:T(8,128)(2,1)}, bf16[512,768]{1,0:T(8,128)(2,1)}, bf16[512,768]{1,0:T(8,128)(2,1)}, f32[8,512]{1,0:T(8,128)}) custom-call(bf16[768,2048]{1,0:T(8,128)(2,1)} %get-tuple-element.43.refs_0_, bf16[768,2048]{1,0:T(8,128)(2,1)} %get-tuple-element.44.refs_1_, bf16[768,768]{1,0:T(8,128)(2,1)} %refs_2_.3, ...), custom_call_target="tpu_custom_call" | custom-call | tf_op jit(solution)/shard_map/pallas_call | solution.py:917
  154.7 3.3 %shard_map.194 = (bf16[1024,768]{1,0:T(8,128)(2,1)}, f32[1024]{0:T(1024)}, f32[768]{0:T(1024)}, f32[1024]{0:T(1024)}, f32[768]{0:T(1024)}) custom-call(bf16[1024,768]{1,0:T(8,128)(2,1)} %get-tuple-element.51.own_ref, bf16[512,768]{1,0:T(8,128)(2,1)} %get-tuple-element.52.left_ref, bf16[512,768]{1,0:T(8,128)(2,1)} %get-tuple-element.53.right_ref, ...), custom_call_target="tpu_custom_call" | custom-call | tf_op jit(solution)/shard_map/pallas_call | solution.py:940
where the time goes:
time: 160 us; the launch traced here: 158 us
  Pallas kernels  157 us (98%)
    pallas_call x1, Pallas kernels, front(): pl.pallas_call(functools.partial(front_kernel, n_head, n_seq, gather), ou...  57.3 us
    pallas_call x1, Pallas kernels, feed(): pl.pallas_call(feed_kernel, grid=(rows // tile,), out_shape=[sds((rows, w...  36.7 us
    pallas_call x1, Pallas kernels, attend_back(): pl.pallas_call(attend_back_kernel, out_shape=outs, in_specs=[SMEM, ANY, A...  30.3 us
    pallas_call x1, Pallas kernels, tail(): pl.pallas_call(functools.partial(tail_kernel, n_head, n_seq), out_shape=o...  29.9 us
    pallas_call x1, Pallas kernels, tail(): pl.pallas_call(functools.partial(finish_kernel, n_head), grid=(rows // SE...  3.33 us

commit v1 on v0

--- a/solution.py
+++ b/solution.py
@@ -603,8 +603,8 @@
     sum_ref[...] = normed
     sweep(0, 1, forward)
     layer_out, inverse_second = norm(sum_ref[...])
-    out_ref[...] = layer_out.T.astype(BF16)
-    grad = norm_back(cot_ref[...].astype(F32).T, layer_out, inverse_second)
+    out_ref[...] = layer_out.astype(BF16).T
+    grad = norm_back(cot_ref[...].T.astype(F32), layer_out, inverse_second)
     sum_ref[...] = grad
     low_ref[...] = grad.astype(BF16)
     sweep(1, 0, lambda piece, upstream: slope_ref[piece, :] * upstream)

time: 160 us -> 161 us (level); the launches traced: 158 us -> 161 us
  Pallas kernels: 157 us -> 160 us
    pallas_call x1, Pallas kernels: 30.3 us -> 36.3 us  [attend_back(): pl.pallas_call(attend_back_kernel, out_shape=outs, in_specs=[SMEM, ANY, A...]
    pallas_call x1, Pallas kernels: 29.9 us -> 26.6 us  [tail(): pl.pallas_call(functools.partial(tail_kernel, n_head, n_seq), out_shape=o...]
where the time goes in v1:
time: 161 us
  Pallas kernels  160 us (99%)
    pallas_call x1, Pallas kernels, front(): pl.pallas_call(functools.partial(front_kernel, n_head, n_seq, gather), ou...  57.3 us
    pallas_call x1, Pallas kernels, feed(): pl.pallas_call(feed_kernel, grid=(rows // tile,), out_shape=[sds((rows, w...  36.5 us
    pallas_call x1, Pallas kernels, attend_back(): pl.pallas_call(attend_back_kernel, out_shape=outs, in_specs=[SMEM, ANY, A...  36.3 us
    pallas_call x1, Pallas kernels, tail(): pl.pallas_call(functools.partial(tail_kernel, n_head, n_seq), out_shape=o...  26.6 us
    pallas_call x1, Pallas kernels, tail(): pl.pallas_call(functools.partial(finish_kernel, n_head), grid=(rows // SE...  3.33 us

profile of v1, /device:TPU:0, one launch (start us, length us, event | category | flops | bytes accessed | tf_op | source)
XLA Modules:
  0.0 160.8 jit_solution(17918331736413619541)
XLA Ops:
  0.6 57.3 %shard_map.190 = (bf16[768,1024]{1,0:T(8,128)(2,1)}, f32[12,1,1024]{2,1,0:T(1,128)}, bf16[768,1024]{1,0:T(8,128)(2,1)}, bf16[768,2048]{1,0:T(8,128)(2,1)}, bf16[...) custom-call(bf16[1024,768]{1,0:T(8,128)(2,1)} %refs_0_.1, ...), custom_call_target="tpu_custom_call" | custom-call | tf_op jit(solution)/shard_map/pallas_call | solution.py:847
  57.9 36.5 %shard_map.191 = (bf16[1024,768]{1,0:T(8,128)(2,1)}, f32[768,1024]{1,0:T(8,128)}, bf16[768,1024]{1,0:T(8,128)(2,1)}, f32[12,1,1024]{2,1,0:T(1,128)}) custom-call(bf16[768,1024]{1,0:T(8,128)(2,1)} %get-tuple-element.33.xt_ref.refs_4_, bf16[768,1024]{1,0:T(8,128)(2,1)} %get-tuple-element.34.ct_ref, bf16[1024,768]{1,0:T(8,128)(2,1)} %cot_ref.1, ...), custom_call_target="tpu_custom_call" | custom-call | tf_op jit(solution)/shard_map/pallas_call | solution.py:866
  94.4 36.3 %shard_map.192 = (bf16[768,1024]{1,0:T(8,128)(2,1)}, bf16[768,2048]{1,0:T(8,128)(2,1)}, bf16[768,2048]{1,0:T(8,128)(2,1)}) custom-call(s32[1,32]{1,0:T(1,128)} %len_ref.1, bf16[768,1024]{1,0:T(8,128)(2,1)} %get-tuple-element.37.qt_hbm, bf16[768,2048]{1,0:T(8,128)(2,1)} %get-tuple-element.38.ke_hbm, bf16[768,2048]{1,0:T(8,128)(2,1)} %get-tuple-element.39.ve_hbm, ...), custom_call_target="tpu_custom_call" | custom-call | tf_op jit(solution)/shard_map/pallas_call | solution.py:891
  130.8 26.6 %shard_map.193 = (bf16[1024,768]{1,0:T(8,128)(2,1)}, bf16[512,768]{1,0:T(8,128)(2,1)}, bf16[512,768]{1,0:T(8,128)(2,1)}, f32[8,512]{1,0:T(8,128)}) custom-call(bf16[768,2048]{1,0:T(8,128)(2,1)} %get-tuple-element.43.refs_0_, bf16[768,2048]{1,0:T(8,128)(2,1)} %get-tuple-element.44.refs_1_, bf16[768,768]{1,0:T(8,128)(2,1)} %refs_2_.3, ...), custom_call_target="tpu_custom_call" | custom-call | tf_op jit(solution)/shard_map/pallas_call | solution.py:917
  157.4 3.3 %shard_map.194 = (bf16[1024,768]{1,0:T(8,128)(2,1)}, f32[1024]{0:T(1024)}, f32[768]{0:T(1024)}, f32[1024]{0:T(1024)}, f32[768]{0:T(1024)}) custom-call(bf16[1024,768]{1,0:T(8,128)(2,1)} %get-tuple-element.51.own_ref, bf16[512,768]{1,0:T(8,128)(2,1)} %get-tuple-element.52.left_ref, bf16[512,768]{1,0:T(8,128)(2,1)} %get-tuple-element.53.right_ref, ...), custom_call_target="tpu_custom_call" | custom-call | tf_op jit(solution)/shard_map/pallas_call | solution.py:940
